TPU v7x, 32 devices: a whole 2x2x4 slice. The times are simulated.
32 devices in a mesh: tau: 2 (over y), wide: 8 (over z, x), narrow: 2 (over core).
Axes of the slice: x: 2, y: 2, z: 4, core: 2. Of those that a mesh axis runs over, the one named last changes fastest.
Arguments:
- integrals: bfloat16 [8, 32, 256, 512], P(None, 'narrow', 'wide'), may hold values from -0.5 to 0.5
- occupied: bfloat16 [4096, 768], P(('tau', 'wide')), parts along dimension 0, may hold values from -0.25 to 0.25
- virtual: bfloat16 [4096, 768], P(('tau', 'wide')), parts along dimension 0, may hold values from -0.25 to 0.25
- pattern: int32 [8, 2, 4], P('wide'), may hold values 0 or 1
Outputs:
- chi: float32 [512, 96], P(('tau', 'wide', 'narrow')), parts along dimension 0
There are 2 independent parts, one for each index of `tau`. A program takes and returns all parts, laid end to end along the dimension named above; an argument that names none is the same for every part. Nothing has to cross between parts.
Inputs may be any that keep to these rules, and one draw needn't show every extreme that they name: `pattern`: 1 where a tile of the integrals is kept, 0 where screening drops it.
All inputs are finite; a program needn't handle non-finite values. No bound on the sum of `pattern` on one device may be relied on, other than what follows from the above.
Results may differ from a plain program's by a relative error of at most 0.0041.
Values may be sent and summed in bfloat16 or wider, within the bound.
A program may use at most 128 MiB of HBM per device.

v0:
```python
import jax
import jax.numpy as jnp
from jax import lax
from jax.sharding import PartitionSpec as P


def passed_along(value, axis, steps):
    count = lax.axis_size(axis)
    pairs = [(source, (source + steps) % count) for source in range(count)]
    return lax.ppermute(value, axis, pairs)


def screened(slab_block, pattern_rows):
    tiles_mu = pattern_rows.shape[0]
    tiles_nu = pattern_rows.shape[1]
    aux_count = slab_block.shape[0]
    tile_width = slab_block.shape[1] // tiles_mu
    shaped = slab_block.reshape(aux_count, tiles_mu, tile_width, tiles_nu, tile_width)
    keep_tile = pattern_rows.astype(slab_block.dtype)[None, :, None, :, None]
    return (shaped * keep_tile).reshape(slab_block.shape)


def windowed(slab_block, here_rows, next_rows):
    aux_count = slab_block.shape[0]
    basis_width = slab_block.shape[1]
    flattened = slab_block.reshape(aux_count * basis_width, 2 * basis_width)
    leading = jnp.dot(flattened[:, :basis_width], here_rows, preferred_element_type=jnp.float32)
    trailing = jnp.dot(
        flattened[:, basis_width:],
        next_rows[:, : 2 * basis_width],
        preferred_element_type=jnp.float32,
    )
    combined = leading + jnp.pad(trailing, ((0, 0), (basis_width, 0)))
    return combined.astype(jnp.bfloat16).reshape(aux_count, basis_width, 3 * basis_width)


def body(integrals, occupied, virtual, pattern):
    basis_width = occupied.shape[0]
    occ_next, virt_next = passed_along((occupied, virtual), "wide", -1)
    slab_block = screened(
        lax.all_to_all(integrals, "wide", split_axis=0, concat_axis=2, tiled=True)[0], pattern[0]
    )
    occ_image = windowed(slab_block, occupied, occ_next)
    virt_image = windowed(slab_block, virtual, virt_next)
    region_all = lax.all_gather(virt_image, "narrow", axis=0, tiled=True)
    received = [
        passed_along(
            region_all[:, :, (offset + 1) * basis_width : (offset + 2) * basis_width],
            "wide",
            offset,
        )
        for offset in (1, -1)
    ]
    paired = jnp.stack([received[0], region_all[:, :, basis_width : 2 * basis_width], received[1]])
    blocks = []
    for column in range(3):
        occ_part = occ_image[:, :, column * basis_width : (column + 1) * basis_width]
        blocks.append(
            lax.dot_general(
                occ_part,
                paired[column],
                (((1, 2), (2, 1)), ((), ())),
                preferred_element_type=jnp.float32,
            )
        )
    return jnp.concatenate(blocks, axis=1)


def solution(mesh):
    in_specs = (
        P(None, "narrow", "wide", None),
        P(("tau", "wide"), None),
        P(("tau", "wide"), None),
        P("wide", None, None),
    )
    out_specs = P(("tau", "wide", "narrow"), None)
    return jax.shard_map(body, mesh=mesh, in_specs=in_specs, out_specs=out_specs, check_vma=False)
```

profile of v0, /device:TPU:0, one launch (start us, length us, event | category | flops | bytes accessed | tf_op | source)
XLA Modules:
  0.0 381.8 jit_solution(4533368190743440357)
XLA Ops:
  6.5 7.4 %all-to-all-start = ((bf16[8,16,32,512]{3,2,1,0:T(8,128)(2,1)}), bf16[8,16,32,512]{3,2,1,0:T(8,128)(2,1)}, u32[]{:S(2)}, u32[]{:S(2)}) async-start(bf16[8,16,32,512]{3,2,1,0:T(8,128)(2,1)} %param.4), calls=%async_computation | async-start | bytes 8388608 | tf_op jit(solution)/shard_map/all_to_all | solution.py:41
  13.9 0.0 all-gather.2.cloned.1.call-start
  14.0 0.0 copy-done.2
  14.0 4.7 %collective-permute-start.1 = (bf16[256,768]{1,0:T(8,128)(2,1)S(1)}, bf16[256,768]{1,0:T(8,128)(2,1)S(1)}, u32[]{:S(2)}, u32[]{:S(2)}) collective-permute-start(bf16[256,768]{1,0:T(8,128)(2,1)S(1)} %copy-done.2), channel_id=1, source_target_pairs={{0,14},{2,0},{4,2},{6,4},{8,6},{10,8},{12,10},{14,12},{1,15},{3,1}... | collective-permute-start | bytes 1179656 | tf_op jit(solution)/shard_map/ppermute | solution.py:10
  18.7 0.0 copy-done.4
  18.7 89.9 %all-to-all-done = bf16[8,16,32,512]{3,2,1,0:T(8,128)(2,1)} async-done(((bf16[8,16,32,512]{3,2,1,0:T(8,128)(2,1)}), bf16[8,16,32,512]{3,2,1,0:T(8,128)(2,1)}, u32[]{:S(2)}, u32[]{:S(2)}) %all-to-all-start) | async-done | bytes 4194336 | tf_op jit(solution)/shard_map/all_to_all | solution.py:41
  108.6 2.7 copy.14
  111.3 1.7 mul.11
  113.0 1.1 bitcast_multiply_fusion
  114.1 0.0 copy-start
  114.1 0.0 collective-permute-done.1
  114.1 1.2 fusion.7
  115.3 0.7 copy-done
  116.0 3.7 add_convert_fusion
  119.7 9.1 %copy.16 = bf16[16,256,768]{1,0,2:T(8,128)(2,1)} copy(bf16[16,256,768]{2,1,0:T(8,128)(2,1)} %bitcast.25) | data formatting | bytes 12582912 | tf_op jit(solution)/shard_map/reshape | solution.py:34
  128.8 0.0 all-gather.2.cloned.1.call-update
  128.8 0.0 copy-start.3
  128.8 31.0 %all-gather.2.cloned.1.call-done = bf16[32,256,768]{1,0,2:T(8,128)(2,1)} async-done(((bf16[16,256,768]{1,0,2:T(8,128)(2,1)}), bf16[32,256,768]{1,0,2:T(8,128)(2,1)}) %all-gather.2.cloned.1.call-update) | async-done | bytes 12582928 | tf_op jit(solution)/shard_map/all_gather | solution.py:45
  159.9 6.6 %fusion.32 = (bf16[32,256,256]{1,0,2:T(8,128)(2,1)}, bf16[32,256,256]{1,0,2:T(8,128)(2,1)}) fusion(bf16[32,256,768]{1,0,2:T(8,128)(2,1)} %all-gather.2.cloned.1.call-done), kind=kLoop, calls=%fused_computation.25 | loop fusion | bytes 16777216 | tf_op jit(solution)/shard_map/slice | solution.py:48
  166.4 1.7 collective-permute-start.2
  168.2 3.0 collective-permute-start.3
  171.2 1.8 collective-permute-start
  173.0 186.2 %collective-permute-done = bf16[256,768]{1,0:T(8,128)(2,1)S(1)} collective-permute-done((bf16[256,768]{1,0:T(8,128)(2,1)S(1)}, bf16[256,768]{1,0:T(8,128)(2,1)S(1)}, u32[]{:S(2)}, u32[]{:S(2)}) %collective-permute-start) | collective-permute-done | bytes 393248 | tf_op jit(solution)/shard_map/ppermute | solution.py:10
  359.2 1.2 fusion.9
  360.4 2.0 add_convert_fusion.1
  362.4 0.8 fusion.33
  363.3 3.6 fusion.19
  366.9 0.0 collective-permute-done.2
  366.9 3.7 fusion.24
  370.6 0.0 collective-permute-done.3
  370.6 3.7 fusion.27
  374.3 0.7 pad_maximum_fusion
  (6 shorter events, 0.0 us)
Async XLA Ops:
  6.5 7.4 %copy-start.2 = (bf16[256,768]{1,0:T(8,128)(2,1)S(1)}, bf16[256,768]{1,0:T(8,128)(2,1)}, u32[]{:S(2)}) copy-start(bf16[256,768]{1,0:T(8,128)(2,1)} %param.6) | copy-start | bytes 1179652
  6.5 12.2 %copy-start.4 = (s32[1,2,4]{2,1,0:T(2,128)S(1)}, s32[1,2,4]{2,1,0:T(2,128)}, u32[]{:S(2)}) copy-start(s32[1,2,4]{2,1,0:T(2,128)} %param.7) | copy-start | bytes 100
  6.5 102.1 %all-to-all-start = ((bf16[8,16,32,512]{3,2,1,0:T(8,128)(2,1)}), bf16[8,16,32,512]{3,2,1,0:T(8,128)(2,1)}, u32[]{:S(2)}, u32[]{:S(2)}) async-start(bf16[8,16,32,512]{3,2,1,0:T(8,128)(2,1)} %param.4), calls=%async_computation | async-start | bytes 8388608 | tf_op jit(solution)/shard_map/all_to_all | solution.py:41
  13.9 146.0 %all-gather.2.cloned.1.call-start = ((), (), s32[]{:S(2)}) async-start(), calls=%async_computation.1 | async-start | bytes 18874368 | tf_op jit(solution)/shard_map/all_gather | solution.py:45
  14.0 100.1 %collective-permute-start.1 = (bf16[256,768]{1,0:T(8,128)(2,1)S(1)}, bf16[256,768]{1,0:T(8,128)(2,1)S(1)}, u32[]{:S(2)}, u32[]{:S(2)}) collective-permute-start(bf16[256,768]{1,0:T(8,128)(2,1)S(1)} %copy-done.2), channel_id=1, source_target_pairs={{0,14},{2,0},{4,2},{6,4},{8,6},{10,8},{12,10},{14,12},{1,15},{3,1}... | collective-permute-start | bytes 1179656 | tf_op jit(solution)/shard_map/ppermute | solution.py:10
  114.1 2.0 copy-start
  128.8 42.4 %copy-start.3 = (bf16[256,768]{1,0:T(8,128)(2,1)S(1)}, bf16[256,768]{1,0:T(8,128)(2,1)}, u32[]{:S(2)}) copy-start(bf16[256,768]{1,0:T(8,128)(2,1)} %param.5) | copy-start | bytes 1179652
  159.9 199.3 %copy-start.1 = (bf16[4096,512]{1,0:T(8,128)(2,1)S(1)}, bf16[4096,512]{1,0:T(8,128)(2,1)}, u32[]{:S(2)}) copy-start(bf16[4096,512]{1,0:T(8,128)(2,1)} %copy-done) | copy-start | bytes 12582916
  166.4 200.5 %collective-permute-start.2 = (bf16[32,256,256]{1,0,2:T(8,128)(2,1)}, bf16[32,256,256]{1,0,2:T(8,128)(2,1)}, u32[]{:S(2)}, u32[]{:S(2)}) collective-permute-start(bf16[32,256,256]{1,0,2:T(8,128)(2,1)} %get-tuple-element.5), channel_id=1, source_target_pairs={{0,2},{2,4},{4,6},{6,8},{8,10},{10,12},{12,14},{14,0},{1,3},{3,5},... | collective-permute-start | bytes 12582920 | tf_op jit(solution)/shard_map/ppermute | solution.py:10
  168.2 202.4 %collective-permute-start.3 = (bf16[32,256,256]{1,0,2:T(8,128)(2,1)}, bf16[32,256,256]{1,0,2:T(8,128)(2,1)}, u32[]{:S(2)}, u32[]{:S(2)}) collective-permute-start(bf16[32,256,256]{1,0,2:T(8,128)(2,1)} %get-tuple-element.6), channel_id=1, source_target_pairs={{0,14},{2,0},{4,2},{6,4},{8,6},{10,8},{12,10},{14,12},{1,15},{3,1}... | collective-permute-start | bytes 12582920 | tf_op jit(solution)/shard_map/ppermute | solution.py:10
  171.2 188.0 %collective-permute-start = (bf16[256,768]{1,0:T(8,128)(2,1)S(1)}, bf16[256,768]{1,0:T(8,128)(2,1)S(1)}, u32[]{:S(2)}, u32[]{:S(2)}) collective-permute-start(bf16[256,768]{1,0:T(8,128)(2,1)S(1)} %copy-done.3), channel_id=1, source_target_pairs={{0,14},{2,0},{4,2},{6,4},{8,6},{10,8},{12,10},{14,12},{1,15},{3,1}... | collective-permute-start | bytes 1179656 | tf_op jit(solution)/shard_map/ppermute | solution.py:10
Sparse Core Ops, SparseCore 0:
  128.9 30.8 all-gather.1
where the time goes:
time: 382 us
  waiting for transfers between devices  307 us (80%)
  local copies, waits for them, and re-layouts  21.5 us (6%)
  matrix products  19.1 us (5%)
  starting transfers between devices  18.7 us (5%)
  between operations  13.5 us (4%)
    ppermute x4, waiting for transfers between devices, passed_along(): return lax.ppermute(value, axis, pairs)  186 us
    all_to_all x1, waiting for transfers between devices, body(): lax.all_to_all(integrals, 'wide', split_axis=0, concat_axis=2, tiled=True)  89.9 us
    all_gather x1, waiting for transfers between devices, body(): region_all = lax.all_gather(virt_image, 'narrow', axis=0, tiled=True)  31 us
    ppermute x4, starting transfers between devices, passed_along(): return lax.ppermute(value, axis, pairs)  11.2 us
    dot_general x3, matrix products, body(): lax.dot_general(occ_part, paired[column], (((1, 2), (2, 1)), ((), ())), p...  11 us
    reshape x1, local copies, waits for them, and re-layouts, windowed(): combined.astype(jnp.bfloat16)  9.09 us
  transfers between devices with their start and end apart: 6, of which 3 were waited for; matrix products, arithmetic and copies ran while one was open for 4% of the time, Pallas kernels for 0%

commit v1 on v0

--- a/solution.py
+++ b/solution.py
@@ -1,6 +1,10 @@
+import functools
+
 import jax
 import jax.numpy as jnp
 from jax import lax
+from jax.experimental import pallas as pl
+from jax.experimental.pallas import tpu as pltpu
 from jax.sharding import PartitionSpec as P
 
 
@@ -34,7 +38,7 @@
     return combined.astype(jnp.bfloat16).reshape(aux_count, basis_width, 3 * basis_width)
 
 
-def body(integrals, occupied, virtual, pattern):
+def plain_body(integrals, occupied, virtual, pattern):
     basis_width = occupied.shape[0]
     occ_next, virt_next = passed_along((occupied, virtual), "wide", -1)
     slab_block = screened(
@@ -66,6 +70,294 @@
     return jnp.concatenate(blocks, axis=1)
 
 
+GROUPS = 2
+NT = (((1,), (1,)), ((), ()))
+
+
+def kernel(
+    width, integrals, occupied, virtual, levels, chi,
+    slab, slab_next, occ_rows, virt_rows, level_mine, level_next,
+    virt_turned, keep, keep_next, occ_img, occ_img_next, virt_img, virt_img_next,
+    sums, edge_out, edge_in,
+    local_sem, first_send, first_recv, tau_send, tau_recv, core_send, core_recv,
+    own_send, own_recv, green_send, green_recv, edge_send, edge_recv,
+):
+    t, k, n = (lax.axis_index(name) for name in ("tau", "wide", "narrow"))
+    own_aux, rows, both = integrals.shape[1:]
+    basis = both // 2
+    part = own_aux // 2
+    step = part // GROUPS
+    other_tau = (1 - t, k, n)
+    other_core = (t, k, 1 - n)
+    behind = lax.rem(k + width - 1, width)
+    ahead = lax.rem(k + 1, width)
+
+    barrier = pltpu.get_barrier_semaphore()
+
+    def greet(distance, carry):
+        pl.semaphore_signal(barrier, inc=1, device_id=(t, lax.rem(k + distance, width), n))
+        return carry
+
+    lax.fori_loop(1, width, greet, 0)
+    pl.semaphore_signal(barrier, inc=1, device_id=other_tau)
+    pl.semaphore_signal(barrier, inc=1, device_id=other_core)
+    pl.semaphore_wait(barrier, width + 1)
+
+    def remote(source, target, send, recv, device):
+        return pltpu.make_async_remote_copy(
+            src_ref=source, dst_ref=target, send_sem=send, recv_sem=recv,
+            device_id=device, device_id_type=pl.DeviceIdType.MESH,
+        )
+
+    def landing(kind, aux, count, source):
+        buffer = (slab, slab_next)[kind]
+        return buffer.at[pl.ds(aux, count), pl.ds(pl.multiple_of(source * rows, rows), rows), :]
+
+    def stored(kind, aux, count, target):
+        if kind == 0:
+            return integrals.at[target, pl.ds(aux, count), :, :]
+        return integrals.at[lax.rem(target + 1, width), pl.ds(aux, count), :, pl.ds(0, basis)]
+
+    def first(kind, group, target, source):
+        aux = part * t + step * group
+        return remote(
+            stored(kind, aux, step, target),
+            landing(kind, own_aux * n + aux, step, source),
+            first_send.at[kind, group, target], first_recv.at[kind, group, source],
+            (t, target, n),
+        )
+
+    def over_tau(kind, group, source, half):
+        block = landing(kind, own_aux * n + part * half + step * group, step, source)
+        return remote(
+            block, block, tau_send.at[kind, group, source], tau_recv.at[kind, group, source], other_tau
+        )
+
+    def over_core(kind, group, source, half, core):
+        block = landing(kind, own_aux * core + part * half + step * group, step, source)
+        which = jnp.where(half == t, 0, 1)
+        return remote(
+            block, block, core_send.at[kind, group, which, source],
+            core_recv.at[kind, group, which, source], other_core,
+        )
+
+    def own_over_core(kind, core):
+        return remote(
+            stored(kind, 0, own_aux, k), landing(kind, own_aux * core, own_aux, k),
+            own_send.at[kind], own_recv.at[kind], other_core,
+        )
+
+    def greens():
+        return (
+            remote(occupied.at[:, pl.ds(0, both)], occ_rows.at[pl.ds(basis, basis), :],
+                   green_send.at[0], green_recv.at[0], (t, behind, n)),
+            remote(virtual.at[:, pl.ds(0, both)], virt_rows.at[pl.ds(basis, basis), :],
+                   green_send.at[1], green_recv.at[1], (t, behind, n)),
+            remote(levels, level_next, green_send.at[2], green_recv.at[2], (t, behind, n)),
+        )
+
+    local = [
+        pltpu.make_async_copy(occupied.at[:, pl.ds(basis, both)], occ_rows.at[pl.ds(0, basis), :], local_sem.at[0]),
+        pltpu.make_async_copy(virtual.at[:, pl.ds(basis, both)], virt_rows.at[pl.ds(0, basis), :], local_sem.at[1]),
+        pltpu.make_async_copy(levels, level_mine, local_sem.at[2]),
+        pltpu.make_async_copy(stored(0, 0, own_aux, k), landing(0, own_aux * n, own_aux, k), local_sem.at[3]),
+        pltpu.make_async_copy(stored(1, 0, own_aux, k), landing(1, own_aux * n, own_aux, k), local_sem.at[4]),
+    ]
+
+    def send_first(group):
+        def at(distance, carry):
+            target = lax.rem(k + distance, width)
+            for kind in (0, 1):
+                first(kind, group, target, k).start()
+            return carry
+        lax.fori_loop(1, width, at, 0)
+
+    for copy in greens():
+        copy.start()
+    send_first(0)
+    for copy in local:
+        copy.start()
+    for kind in (0, 1):
+        own_over_core(kind, n).start()
+    for group in range(1, GROUPS):
+        send_first(group)
+
+    for copy in local:
+        copy.wait()
+    for copy in greens():
+        copy.wait_recv()
+
+    tile = 128
+    for target, level, columns in ((keep, level_mine, 4), (keep_next, level_next, 2)):
+        for m in range(2):
+            for j in range(columns):
+                value = level[pl.ds(4 * m + j, 1), :]
+                target[pl.ds(m * tile, tile), pl.ds(j * tile, tile)] = jnp.broadcast_to(
+                    value, (tile, tile)).astype(jnp.bfloat16)
+    virt_turned[...] = virt_rows[...].astype(jnp.float32).T.astype(jnp.bfloat16)
+
+    def relay(group):
+        def from_first(distance):
+            source = lax.rem(k + width - distance, width)
+            for kind in (0, 1):
+                first(kind, group, source, source).wait_recv()
+                over_tau(kind, group, source, t).start()
+                over_core(kind, group, source, t, n).start()
+
+        def from_tau(distance):
+            source = lax.rem(k + width - distance, width)
+            for kind in (0, 1):
+                over_tau(kind, group, source, 1 - t).wait_recv()
+                over_core(kind, group, source, 1 - t, n).start()
+
+        def at(distance, carry):
+            from_first(distance)
+            from_tau(distance - 1)
+            return carry
+
+        from_first(1)
+        lax.fori_loop(2, width, at, 0)
+        from_tau(width - 1)
+
+        def gathered(distance, carry):
+            source = lax.rem(k + width - distance, width)
+            for kind in (0, 1):
+                over_core(kind, group, source, t, 1 - n).wait_recv()
+                over_core(kind, group, source, 1 - t, 1 - n).wait_recv()
+            return carry
+
+        lax.fori_loop(1, width, gathered, 0)
+
+    def images(group):
+        def virt_at(step_index, carry):
+            aux = (step_index // step) * part + step * group + step_index % step
+            piece = slab[aux] * keep[...]
+            virt_img[aux] = lax.dot_general(
+                virt_turned[...], piece, NT, preferred_element_type=jnp.float32).astype(jnp.bfloat16)
+            piece = slab_next[aux] * keep_next[...]
+            virt_img_next[aux] = lax.dot_general(
+                virt_turned[pl.ds(0, basis), pl.ds(basis, basis)], piece, NT,
+                preferred_element_type=jnp.float32).astype(jnp.bfloat16)
+            return carry
+
+        lax.fori_loop(0, 4 * step, virt_at, 0)
+
+        def occ_at(step_index, carry):
+            mine = (step_index // step) * part + step * group + step_index % step
+            aux = own_aux * n + mine
+            occ_img[mine] = jnp.dot(
+                slab[aux] * keep[...], occ_rows[...],
+                preferred_element_type=jnp.float32).astype(jnp.bfloat16)
+            occ_img_next[mine] = jnp.dot(
+                slab_next[aux] * keep_next[...], occ_rows[pl.ds(basis, basis), pl.ds(0, basis)],
+                preferred_element_type=jnp.float32).astype(jnp.bfloat16)
+            return carry
+
+        lax.fori_loop(0, 2 * step, occ_at, 0)
+
+    for group in range(GROUPS):
+        relay(group)
+        if group == 0:
+            for kind in (0, 1):
+                own_over_core(kind, 1 - n).wait_recv()
+        images(group)
+
+    packed = 16
+    all_aux = 2 * own_aux
+
+    def paired(left, left_column, right, right_row):
+        sums[...] = jnp.zeros_like(sums)
+
+        def at(index, carry):
+            start = pl.multiple_of(index * packed, packed)
+            one = left[:, pl.ds(start, packed), pl.ds(left_column, basis)]
+            two = right[:, pl.ds(right_row + start, packed), :]
+            sums[...] += lax.dot_general(
+                one.reshape(own_aux * packed, basis), two.reshape(all_aux * packed, basis), NT,
+                preferred_element_type=jnp.float32)
+            return carry
+
+        lax.fori_loop(0, basis // packed, at, 0)
+        shape = sums.shape
+        equal = (lax.broadcasted_iota(jnp.int32, shape, 0) % packed
+                 == lax.broadcasted_iota(jnp.int32, shape, 1) % packed)
+        kept = jnp.where(equal, sums[...], 0.0).reshape(own_aux, packed, shape[1]).sum(axis=1)
+        spread = (shape[1], 128)
+        pick = (lax.broadcasted_iota(jnp.int32, spread, 0) // packed
+                == lax.broadcasted_iota(jnp.int32, spread, 1)).astype(jnp.float32)
+        return jnp.dot(kept, pick, precision=lax.Precision.HIGHEST, preferred_element_type=jnp.float32)
+
+    edge_out[...] = paired(occ_img_next, 0, virt_img, basis)
+    edge = remote(edge_out, edge_in, edge_send, edge_recv, (t, ahead, n))
+    edge.start()
+    same = paired(occ_img, 0, virt_img, 0)
+    following = paired(occ_img, basis, virt_img_next, 0)
+    edge.wait()
+    chi[...] = jnp.concatenate(
+        [edge_in[:, :all_aux], same[:, :all_aux], following[:, :all_aux]], axis=1)
+
+    for group in range(GROUPS):
+        def drained(distance, carry):
+            other = lax.rem(k + distance, width)
+            for kind in (0, 1):
+                first(kind, group, other, k).wait_send()
+                over_tau(kind, group, other, t).wait_send()
+                over_core(kind, group, other, t, n).wait_send()
+                over_core(kind, group, other, 1 - t, n).wait_send()
+            return carry
+        lax.fori_loop(1, width, drained, 0)
+    for kind in (0, 1):
+        own_over_core(kind, n).wait_send()
+    for copy in greens():
+        copy.wait_send()
+
+
+def fused_body(width, integrals, occupied, virtual, pattern):
+    own_aux, rows, both = integrals.shape[1:]
+    basis = both // 2
+    levels = jnp.broadcast_to(pattern.reshape(-1, 1).astype(jnp.float32), (pattern.size, 128))
+    bf16, f32 = jnp.bfloat16, jnp.float32
+    dma = pltpu.SemaphoreType.DMA
+    grid = (2, GROUPS, width)
+    anywhere = pl.BlockSpec(memory_space=pl.ANY)
+    return pl.pallas_call(
+        functools.partial(kernel, width),
+        out_shape=jax.ShapeDtypeStruct((own_aux, 6 * own_aux), f32),
+        in_specs=[anywhere] * 4,
+        out_specs=pl.BlockSpec(memory_space=pltpu.VMEM),
+        scratch_shapes=[
+            pltpu.VMEM((2 * own_aux, basis, both), bf16),
+            pltpu.VMEM((2 * own_aux, basis, basis), bf16),
+            pltpu.VMEM((both, both), bf16),
+            pltpu.VMEM((both, both), bf16),
+            pltpu.VMEM(levels.shape, f32),
+            pltpu.VMEM(levels.shape, f32),
+            pltpu.VMEM((both, both), bf16),
+            pltpu.VMEM((basis, both), bf16),
+            pltpu.VMEM((basis, basis), bf16),
+            pltpu.VMEM((own_aux, basis, both), bf16),
+            pltpu.VMEM((own_aux, basis, basis), bf16),
+            pltpu.VMEM((2 * own_aux, both, basis), bf16),
+            pltpu.VMEM((2 * own_aux, basis, basis), bf16),
+            pltpu.VMEM((16 * own_aux, 32 * own_aux), f32),
+            pltpu.VMEM((own_aux, 128), f32),
+            pltpu.VMEM((own_aux, 128), f32),
+            dma((5,)), dma(grid), dma(grid), dma(grid), dma(grid),
+            dma((2, GROUPS, 2, width)), dma((2, GROUPS, 2, width)),
+            dma((2,)), dma((2,)), dma((3,)), dma((3,)), dma(()), dma(()),
+        ],
+        compiler_params=pltpu.CompilerParams(
+            collective_id=0, has_side_effects=True, vmem_limit_bytes=56 * 2**20
+        ),
+    )(integrals, occupied, virtual, levels)
+
+
+def body(sizes, integrals, occupied, virtual, pattern):
+    if sizes["tau"] == 2 and sizes["narrow"] == 2 and integrals.shape[2] % 16 == 0:
+        return fused_body(sizes["wide"], integrals, occupied, virtual, pattern)
+    return plain_body(integrals, occupied, virtual, pattern)
+
+
 def solution(mesh):
     in_specs = (
         P(None, "narrow", "wide", None),
@@ -74,4 +366,7 @@
         P("wide", None, None),
     )
     out_specs = P(("tau", "wide", "narrow"), None)
-    return jax.shard_map(body, mesh=mesh, in_specs=in_specs, out_specs=out_specs, check_vma=False)
+    return jax.shard_map(
+        functools.partial(body, dict(mesh.shape)),
+        mesh=mesh, in_specs=in_specs, out_specs=out_specs, check_vma=False,
+    )

time: 382 us -> 142 us (0.37)
  the two profiles are of different devices: /device:TPU:0 before, /device:TPU:11 now
where the time goes in v1:
time: 142 us; the launch traced here: 141 us
  Pallas kernels  139 us (98%)
  local copies, waits for them, and re-layouts  2.04 us (1%)
    pallas_call x1, Pallas kernels, fused_body(): pl.pallas_call(functools.partial(kernel, width), out_shape=jax.ShapeDtype...  139 us

profile of v1, /device:TPU:11, one launch (start us, length us, event | category | flops | bytes accessed | tf_op | source)
XLA Modules:
  0.0 141.4 jit_solution(11718624201555155756)
XLA Ops:
  0.0 0.7 convert_element_type.11
  0.7 0.1 convert_element_type.12
  0.8 0.7 broadcast_in_dim.2.levels
  1.4 138.7 %shard_map.46 = f32[16,96]{1,0:T(8,128)} custom-call(bf16[8,16,32,512]{3,2,1,0:T(8,128)(2,1)} %integrals.1, bf16[256,768]{1,0:T(8,128)(2,1)} %occupied.1, bf16[256,768]{1,0:T(8,128)(2,1)} %virtual.1, f32[8,128]{1,0:T(8,128)} %broadcast_in_dim.2.levels), custom_call_target="tpu_custom_call" | custom-call | tf_op jit(solution)/shard_map/pallas_call | solution.py:323
  140.1 1.3 copy.6

commit v2 on v1

--- a/solution.py
+++ b/solution.py
@@ -71,6 +71,8 @@
 
 
 GROUPS = 2
+LAG = 1
+SPAN = 4
 NT = (((1,), (1,)), ((), ()))
 
 
@@ -80,7 +82,7 @@
     virt_turned, keep, keep_next, occ_img, occ_img_next, virt_img, virt_img_next,
     sums, edge_out, edge_in,
     local_sem, first_send, first_recv, tau_send, tau_recv, core_send, core_recv,
-    own_send, own_recv, green_send, green_recv, edge_send, edge_recv,
+    own_send, own_recv, green_send, green_recv, edge_send, edge_recv, pair_send,
 ):
     t, k, n = (lax.axis_index(name) for name in ("tau", "wide", "narrow"))
     own_aux, rows, both = integrals.shape[1:]
@@ -147,14 +149,25 @@
             own_send.at[kind], own_recv.at[kind], other_core,
         )
 
+    def green_rows(core):
+        return pl.ds(pl.multiple_of(core * (basis // 2), basis // 2), basis // 2)
+
+    def green_landing(rows_ref, core):
+        return rows_ref.at[pl.ds(pl.multiple_of(basis + core * (basis // 2), basis // 2), basis // 2), :]
+
     def greens():
-        return (
-            remote(occupied.at[:, pl.ds(0, both)], occ_rows.at[pl.ds(basis, basis), :],
-                   green_send.at[0], green_recv.at[0], (t, behind, n)),
-            remote(virtual.at[:, pl.ds(0, both)], virt_rows.at[pl.ds(basis, basis), :],
-                   green_send.at[1], green_recv.at[1], (t, behind, n)),
-            remote(levels, level_next, green_send.at[2], green_recv.at[2], (t, behind, n)),
-        )
+        return [
+            remote(green.at[green_rows(n), pl.ds(0, both)], green_landing(rows_ref, n),
+                   green_send.at[i], green_recv.at[i], (t, behind, n))
+            for i, (green, rows_ref) in enumerate(((occupied, occ_rows), (virtual, virt_rows)))
+        ] + [remote(levels, level_next, green_send.at[2], green_recv.at[2], (t, behind, n))]
+
+    def greens_over_core(core):
+        return [
+            remote(green_landing(rows_ref, core), green_landing(rows_ref, core),
+                   green_send.at[3 + i], green_recv.at[3 + i], other_core)
+            for i, rows_ref in enumerate((occ_rows, virt_rows))
+        ]
 
     local = [
         pltpu.make_async_copy(occupied.at[:, pl.ds(basis, both)], occ_rows.at[pl.ds(0, basis), :], local_sem.at[0]),
@@ -164,11 +177,28 @@
         pltpu.make_async_copy(stored(1, 0, own_aux, k), landing(1, own_aux * n, own_aux, k), local_sem.at[4]),
     ]
 
+    def direct(target):
+        return jnp.logical_or(target % 2 == 1, target == k - 1)
+
+    def passes_on(source):
+        return jnp.logical_and(k % 2 == 1, source != k - 1)
+
+    def over_pair(group, source):
+        aux = own_aux * n + part * t + step * group
+        here = pl.ds(pl.multiple_of(source * rows, rows), rows)
+        return remote(
+            slab.at[pl.ds(aux, step), here, pl.ds(0, basis)], landing(1, aux, step, source),
+            pair_send.at[group, source], first_recv.at[1, group, source], (t, behind, n),
+        )
+
     def send_first(group):
         def at(distance, carry):
             target = lax.rem(k + distance, width)
-            for kind in (0, 1):
-                first(kind, group, target, k).start()
+            first(0, group, target, k).start()
+
+            @pl.when(direct(target))
+            def _():
+                first(1, group, target, k).start()
             return carry
         lax.fori_loop(1, width, at, 0)
 
@@ -186,106 +216,131 @@
         copy.wait()
     for copy in greens():
         copy.wait_recv()
-
-    tile = 128
-    for target, level, columns in ((keep, level_mine, 4), (keep_next, level_next, 2)):
-        for m in range(2):
+    for copy in greens_over_core(n):
+        copy.start()
+    for copy in greens_over_core(1 - n):
+        copy.wait_recv()
+
+    tiles = levels.shape[0]
+    tile = basis // tiles
+    for target, level, columns in ((keep, level_mine, 2 * tiles), (keep_next, level_next, tiles)):
+        for m in range(tiles):
             for j in range(columns):
-                value = level[pl.ds(4 * m + j, 1), :]
+                value = level[pl.ds(m, 1), pl.ds(j, 1)].astype(jnp.float32)
                 target[pl.ds(m * tile, tile), pl.ds(j * tile, tile)] = jnp.broadcast_to(
                     value, (tile, tile)).astype(jnp.bfloat16)
     virt_turned[...] = virt_rows[...].astype(jnp.float32).T.astype(jnp.bfloat16)
 
-    def relay(group):
-        def from_first(distance):
-            source = lax.rem(k + width - distance, width)
-            for kind in (0, 1):
-                first(kind, group, source, source).wait_recv()
-                over_tau(kind, group, source, t).start()
-                over_core(kind, group, source, t, n).start()
-
-        def from_tau(distance):
-            source = lax.rem(k + width - distance, width)
-            for kind in (0, 1):
-                over_tau(kind, group, source, 1 - t).wait_recv()
-                over_core(kind, group, source, 1 - t, n).start()
-
+    def from_first(group, distance):
+        source = lax.rem(k + width - distance, width)
+        for kind in (0, 1):
+            first(kind, group, source, source).wait_recv()
+            over_tau(kind, group, source, t).start()
+            if kind == 0:
+                @pl.when(passes_on(source))
+                def _():
+                    over_pair(group, source).start()
+            over_core(kind, group, source, t, n).start()
+
+    def from_tau(group, distance):
+        source = lax.rem(k + width - distance, width)
+        for kind in (0, 1):
+            over_tau(kind, group, source, 1 - t).wait_recv()
+            over_core(kind, group, source, 1 - t, n).start()
+
+    def relay(group, low, high):
         def at(distance, carry):
-            from_first(distance)
-            from_tau(distance - 1)
-            return carry
-
-        from_first(1)
-        lax.fori_loop(2, width, at, 0)
-        from_tau(width - 1)
-
-        def gathered(distance, carry):
+            @pl.when(distance < width)
+            def _():
+                from_first(group, distance)
+
+            @pl.when(distance > LAG)
+            def _():
+                from_tau(group, distance - LAG)
+            return carry
+
+        lax.fori_loop(low, high, at, 0)
+
+    relay_steps = width - 1 + LAG
+
+    def gathered(group):
+        def at(distance, carry):
             source = lax.rem(k + width - distance, width)
             for kind in (0, 1):
                 over_core(kind, group, source, t, 1 - n).wait_recv()
                 over_core(kind, group, source, 1 - t, 1 - n).wait_recv()
             return carry
 
-        lax.fori_loop(1, width, gathered, 0)
+        lax.fori_loop(1, width, at, 0)
+
+    def virt_images(aux, piece, piece_next):
+        virt_img[aux] = lax.dot_general(
+            virt_turned[...], piece, NT, preferred_element_type=jnp.float32).astype(jnp.bfloat16)
+        virt_img_next[aux] = lax.dot_general(
+            virt_turned[pl.ds(0, basis), pl.ds(basis, basis)], piece_next, NT,
+            preferred_element_type=jnp.float32).astype(jnp.bfloat16)
 
     def images(group):
-        def virt_at(step_index, carry):
-            aux = (step_index // step) * part + step * group + step_index % step
+        turns = 2 * step
+
+        def at(turn, carry):
+            if group + 1 < GROUPS:
+                relay(group + 1, 1 + turn * relay_steps // turns, 1 + (turn + 1) * relay_steps // turns)
+            mine = (turn // step) * part + step * group + turn % step
+            theirs = own_aux * (1 - n) + mine
+            virt_images(theirs, slab[theirs] * keep[...], slab_next[theirs] * keep_next[...])
+            aux = own_aux * n + mine
             piece = slab[aux] * keep[...]
-            virt_img[aux] = lax.dot_general(
-                virt_turned[...], piece, NT, preferred_element_type=jnp.float32).astype(jnp.bfloat16)
-            piece = slab_next[aux] * keep_next[...]
-            virt_img_next[aux] = lax.dot_general(
-                virt_turned[pl.ds(0, basis), pl.ds(basis, basis)], piece, NT,
+            piece_next = slab_next[aux] * keep_next[...]
+            virt_images(aux, piece, piece_next)
+            occ_img[mine] = jnp.dot(
+                piece, occ_rows[...], preferred_element_type=jnp.float32).astype(jnp.bfloat16)
+            occ_img_next[mine] = jnp.dot(
+                piece_next, occ_rows[pl.ds(basis, basis), pl.ds(0, basis)],
                 preferred_element_type=jnp.float32).astype(jnp.bfloat16)
             return carry
 
-        lax.fori_loop(0, 4 * step, virt_at, 0)
-
-        def occ_at(step_index, carry):
-            mine = (step_index // step) * part + step * group + step_index % step
-            aux = own_aux * n + mine
-            occ_img[mine] = jnp.dot(
-                slab[aux] * keep[...], occ_rows[...],
-                preferred_element_type=jnp.float32).astype(jnp.bfloat16)
-            occ_img_next[mine] = jnp.dot(
-                slab_next[aux] * keep_next[...], occ_rows[pl.ds(basis, basis), pl.ds(0, basis)],
-                preferred_element_type=jnp.float32).astype(jnp.bfloat16)
-            return carry
-
-        lax.fori_loop(0, 2 * step, occ_at, 0)
-
+        lax.fori_loop(0, turns, at, 0)
+
+    relay(0, 1, relay_steps + 1)
+    for kind in (0, 1):
+        own_over_core(kind, 1 - n).wait_recv()
     for group in range(GROUPS):
-        relay(group)
-        if group == 0:
-            for kind in (0, 1):
-                own_over_core(kind, 1 - n).wait_recv()
+        gathered(group)
         images(group)
 
     packed = 16
     all_aux = 2 * own_aux
 
     def paired(left, left_column, right, right_row):
-        sums[...] = jnp.zeros_like(sums)
-
-        def at(index, carry):
+        def at(index, total):
             start = pl.multiple_of(index * packed, packed)
             one = left[:, pl.ds(start, packed), pl.ds(left_column, basis)]
             two = right[:, pl.ds(right_row + start, packed), :]
-            sums[...] += lax.dot_general(
-                one.reshape(own_aux * packed, basis), two.reshape(all_aux * packed, basis), NT,
+            return total + lax.dot_general(
+                two.reshape(all_aux * packed, basis), one.reshape(own_aux * packed, basis), NT,
                 preferred_element_type=jnp.float32)
-            return carry
-
-        lax.fori_loop(0, basis // packed, at, 0)
+
+        sums[...] = jnp.zeros_like(sums)
+
+        def several(index, carry):
+            total = sums[...]
+            for inner in range(SPAN):
+                total = at(index * SPAN + inner, total)
+            sums[...] = total
+            return carry
+
+        lax.fori_loop(0, basis // packed // SPAN, several, 0)
         shape = sums.shape
-        equal = (lax.broadcasted_iota(jnp.int32, shape, 0) % packed
-                 == lax.broadcasted_iota(jnp.int32, shape, 1) % packed)
-        kept = jnp.where(equal, sums[...], 0.0).reshape(own_aux, packed, shape[1]).sum(axis=1)
-        spread = (shape[1], 128)
-        pick = (lax.broadcasted_iota(jnp.int32, spread, 0) // packed
+        equal = ((lax.broadcasted_iota(jnp.int32, shape, 0) ^ lax.broadcasted_iota(jnp.int32, shape, 1))
+                 & (packed - 1)) == 0
+        kept = jnp.where(equal, sums[...], 0.0).reshape(all_aux, packed, shape[1]).sum(axis=1)
+        spread = (shape[1], own_aux)
+        pick = ((lax.broadcasted_iota(jnp.int32, spread, 0) >> 4)
                 == lax.broadcasted_iota(jnp.int32, spread, 1)).astype(jnp.float32)
-        return jnp.dot(kept, pick, precision=lax.Precision.HIGHEST, preferred_element_type=jnp.float32)
+        return lax.dot_general(
+            pick, kept, (((0,), (1,)), ((), ())),
+            precision=lax.Precision.HIGHEST, preferred_element_type=jnp.float32)
 
     edge_out[...] = paired(occ_img_next, 0, virt_img, basis)
     edge = remote(edge_out, edge_in, edge_send, edge_recv, (t, ahead, n))
@@ -294,13 +349,22 @@
     following = paired(occ_img, basis, virt_img_next, 0)
     edge.wait()
     chi[...] = jnp.concatenate(
-        [edge_in[:, :all_aux], same[:, :all_aux], following[:, :all_aux]], axis=1)
+        [edge_in[...], same, following], axis=1)
 
     for group in range(GROUPS):
         def drained(distance, carry):
             other = lax.rem(k + distance, width)
+            first(0, group, other, k).wait_send()
+
+            @pl.when(direct(other))
+            def _():
+                first(1, group, other, k).wait_send()
+
+            @pl.when(passes_on(other))
+            def _():
+                over_pair(group, other).wait_send()
+
             for kind in (0, 1):
-                first(kind, group, other, k).wait_send()
                 over_tau(kind, group, other, t).wait_send()
                 over_core(kind, group, other, t, n).wait_send()
                 over_core(kind, group, other, 1 - t, n).wait_send()
@@ -308,14 +372,14 @@
         lax.fori_loop(1, width, drained, 0)
     for kind in (0, 1):
         own_over_core(kind, n).wait_send()
-    for copy in greens():
+    for copy in greens() + greens_over_core(n):
         copy.wait_send()
 
 
 def fused_body(width, integrals, occupied, virtual, pattern):
     own_aux, rows, both = integrals.shape[1:]
     basis = both // 2
-    levels = jnp.broadcast_to(pattern.reshape(-1, 1).astype(jnp.float32), (pattern.size, 128))
+    levels = pattern[0]
     bf16, f32 = jnp.bfloat16, jnp.float32
     dma = pltpu.SemaphoreType.DMA
     grid = (2, GROUPS, width)
@@ -330,8 +394,8 @@
             pltpu.VMEM((2 * own_aux, basis, basis), bf16),
             pltpu.VMEM((both, both), bf16),
             pltpu.VMEM((both, both), bf16),
-            pltpu.VMEM(levels.shape, f32),
-            pltpu.VMEM(levels.shape, f32),
+            pltpu.VMEM(levels.shape, levels.dtype),
+            pltpu.VMEM(levels.shape, levels.dtype),
             pltpu.VMEM((both, both), bf16),
             pltpu.VMEM((basis, both), bf16),
             pltpu.VMEM((basis, basis), bf16),
@@ -339,12 +403,12 @@
             pltpu.VMEM((own_aux, basis, basis), bf16),
             pltpu.VMEM((2 * own_aux, both, basis), bf16),
             pltpu.VMEM((2 * own_aux, basis, basis), bf16),
-            pltpu.VMEM((16 * own_aux, 32 * own_aux), f32),
-            pltpu.VMEM((own_aux, 128), f32),
-            pltpu.VMEM((own_aux, 128), f32),
+            pltpu.VMEM((32 * own_aux, 16 * own_aux), f32),
+            pltpu.VMEM((own_aux, 2 * own_aux), f32),
+            pltpu.VMEM((own_aux, 2 * own_aux), f32),
             dma((5,)), dma(grid), dma(grid), dma(grid), dma(grid),
             dma((2, GROUPS, 2, width)), dma((2, GROUPS, 2, width)),
-            dma((2,)), dma((2,)), dma((3,)), dma((3,)), dma(()), dma(()),
+            dma((2,)), dma((2,)), dma((5,)), dma((5,)), dma(()), dma(()), dma((GROUPS, width)),
         ],
         compiler_params=pltpu.CompilerParams(
             collective_id=0, has_side_effects=True, vmem_limit_bytes=56 * 2**20
@@ -353,7 +417,7 @@
 
 
 def body(sizes, integrals, occupied, virtual, pattern):
-    if sizes["tau"] == 2 and sizes["narrow"] == 2 and integrals.shape[2] % 16 == 0:
+    if sizes["tau"] == 2 and sizes["narrow"] == 2 and integrals.shape[2] % 16 == 0 and sizes["wide"] % 2 == 0:
         return fused_body(sizes["wide"], integrals, occupied, virtual, pattern)
     return plain_body(integrals, occupied, virtual, pattern)
 

time: 142 us -> 114 us (0.80)
  the two profiles are of different devices: /device:TPU:11 before, /device:TPU:0 now
where the time goes in v2:
time: 114 us
  Pallas kernels  112 us (98%)
  local copies, waits for them, and re-layouts  1.3 us (1%)
    pallas_call x1, Pallas kernels, fused_body(): pl.pallas_call(functools.partial(kernel, width), out_shape=jax.ShapeDtype...  112 us

profile of v2, /device:TPU:0, one launch (start us, length us, event | category | flops | bytes accessed | tf_op | source)
XLA Modules:
  0.0 113.6 jit_solution(5424304417694524706)
XLA Ops:
  0.0 112.3 %shard_map.46 = f32[16,96]{1,0:T(8,128)} custom-call(bf16[8,16,32,512]{3,2,1,0:T(8,128)(2,1)} %integrals.1, bf16[256,768]{1,0:T(8,128)(2,1)} %occupied.1, bf16[256,768]{1,0:T(8,128)(2,1)} %virtual.1, s32[2,4]{1,0:T(2,128)} %bitcast.1), custom_call_target="tpu_custom_call" | custom-call | tf_op jit(solution)/shard_map/pallas_call | solution.py:387
  112.3 1.3 %copy.6 = f32[16,96]{1,0:T(8,128)} copy(f32[16,96]{1,0:T(8,128)} %shard_map.46) | data formatting | bytes 12288

commit v3 on v2

--- a/solution.py
+++ b/solution.py
@@ -71,8 +71,8 @@
 
 
 GROUPS = 2
-LAG = 1
-SPAN = 4
+LAG = 2
+SPAN = 16
 NT = (((1,), (1,)), ((), ()))
 
 

time: 114 us -> 113 us (level)
  no operation moved by 1% of the time
where the time goes in v3:
time: 113 us
  Pallas kernels  112 us (99%)
  local copies, waits for them, and re-layouts  1.3 us (1%)
    pallas_call x1, Pallas kernels, fused_body(): pl.pallas_call(functools.partial(kernel, width), out_shape=jax.ShapeDtype...  112 us

profile of v3, /device:TPU:0, one launch (start us, length us, event | category | flops | bytes accessed | tf_op | source)
XLA Modules:
  0.0 113.2 jit_solution(18432285613135310475)
XLA Ops:
  0.0 111.9 %shard_map.46 = f32[16,96]{1,0:T(8,128)} custom-call(bf16[8,16,32,512]{3,2,1,0:T(8,128)(2,1)} %integrals.1, bf16[256,768]{1,0:T(8,128)(2,1)} %occupied.1, bf16[256,768]{1,0:T(8,128)(2,1)} %virtual.1, s32[2,4]{1,0:T(2,128)} %bitcast.1), custom_call_target="tpu_custom_call" | custom-call | tf_op jit(solution)/shard_map/pallas_call | solution.py:387
  111.9 1.3 %copy.6 = f32[16,96]{1,0:T(8,128)} copy(f32[16,96]{1,0:T(8,128)} %shard_map.46) | data formatting | bytes 12288
